TPU v7x, 32 devices: a whole 2x2x4 slice. The times are simulated.
32 devices in a mesh: grp: 2 (over y), atoms: 4 (over z), vec: 2 (over x), sub: 2 (over core).
Axes of the slice: x: 2, y: 2, z: 4, core: 2. Of those that a mesh axis runs over, the one named last changes fastest.
Arguments:
- t_prev: float32 [256, 12288], P('grp', ('atoms', 'vec', 'sub')), parts along dimension 0, may hold values from -6 to 6
- t_cur: float32 [256, 12288], P('grp', ('atoms', 'vec', 'sub')), parts along dimension 0, may hold values from -6 to 6
- diag_blocks: bfloat16 [64, 384, 384], P(('grp', 'atoms', 'vec', 'sub')), parts along dimension 0, as said below
- upper_half_blocks: bfloat16 [320, 384, 384], P(('grp', 'atoms', 'vec', 'sub')), parts along dimension 0, may hold values from -0.046875 to 0.046875
- offsets: int32 [64, 5], P(('grp', 'atoms', 'vec', 'sub')), parts along dimension 0, may hold values from 1 to 8, as said below
Outputs:
- t_one: float32 [256, 12288], P('grp', ('atoms', 'vec', 'sub')), parts along dimension 0
- t_two: float32 [256, 12288], P('grp', ('atoms', 'vec', 'sub')), parts along dimension 0
There are 2 independent parts, one for each index of `grp`. A program takes and returns all parts, laid end to end along the dimension named above; each array names one. Nothing has to cross between parts.
Inputs may be any that keep to these rules, and one draw needn't show every extreme that they name: Each block row names 5 different offsets; block row 0 names 8. `diag_blocks`: each diagonal block is symmetric.
All inputs are finite; a program needn't handle non-finite values.
Results may differ from a plain program's by a relative error of at most 0.0047.
Values may be sent and summed in bfloat16 or wider, within the bound.
A program may use at most 64 MiB of HBM per device.

v0:
```python
import jax
import jax.numpy as jnp
from jax import lax
from jax.sharding import PartitionSpec as P

HOPS = 4


def passed_along(block, axis, distance):
    devices = range(lax.axis_size(axis))
    route = [((i - distance) % len(devices), i) for i in devices]
    return lax.ppermute(block, axis, route)


def apply_operator(current, diag_blocks, upper_half_blocks, offsets):
    vectors = current.shape[0]
    blocks_of_row = diag_blocks.shape[0]
    block_size = diag_blocks.shape[1]
    slot_count = offsets.shape[1]
    window = (HOPS + 1) * blocks_of_row
    sendable = jnp.transpose(
        current.astype(jnp.bfloat16).reshape(vectors, blocks_of_row, block_size), (1, 0, 2)
    )
    stored = upper_half_blocks.reshape(blocks_of_row, slot_count, block_size, block_size)
    slot_window = jnp.arange(blocks_of_row, dtype=jnp.int32)[:, None] + offsets
    selector = slot_window[:, :, None] == jnp.arange(window, dtype=jnp.int32)[None, None, :]
    transposed = jnp.einsum("rkab,rva->rkvb", stored, sendable, preferred_element_type=jnp.float32)
    grouped = jnp.einsum(
        "rkw,rkvb->wvb", selector.astype(jnp.float32), transposed, precision=lax.Precision.HIGHEST
    ).astype(jnp.bfloat16)
    result = jnp.einsum("rab,rvb->rva", diag_blocks, sendable, preferred_element_type=jnp.float32)
    result = result + grouped[:blocks_of_row].astype(jnp.float32)
    for distance in range(1, HOPS + 1):
        outgoing = grouped[distance * blocks_of_row : (distance + 1) * blocks_of_row]
        arrived = passed_along(outgoing, ("atoms", "vec", "sub"), distance)
        result = result + arrived.astype(jnp.float32)
    groups = [sendable]
    for distance in range(1, HOPS + 1):
        groups.append(passed_along(sendable, ("atoms", "vec", "sub"), -distance))
    neighbor_blocks = jnp.concatenate(groups, axis=0)
    column_blocks = jnp.einsum(
        "rkw,wvb->rkvb",
        selector.astype(jnp.bfloat16),
        neighbor_blocks,
        preferred_element_type=jnp.float32,
    ).astype(jnp.bfloat16)
    result = result + jnp.einsum(
        "rkab,rkvb->rva", stored, column_blocks, preferred_element_type=jnp.float32
    )
    return jnp.transpose(result, (1, 0, 2)).reshape(vectors, blocks_of_row * block_size)


def local(t_prev, t_cur, diag_blocks, upper_half_blocks, offsets):
    t_one = 2.0 * apply_operator(t_cur, diag_blocks, upper_half_blocks, offsets) - t_prev
    t_two = 2.0 * apply_operator(t_one, diag_blocks, upper_half_blocks, offsets) - t_cur
    return (t_one, t_two)


def solution(mesh):
    in_specs = (
        P("grp", ("atoms", "vec", "sub")),
        P("grp", ("atoms", "vec", "sub")),
        P(("grp", "atoms", "vec", "sub"), None, None),
        P(("grp", "atoms", "vec", "sub"), None, None),
        P(("grp", "atoms", "vec", "sub"), None),
    )
    out_specs = (P("grp", ("atoms", "vec", "sub")), P("grp", ("atoms", "vec", "sub")))
    return jax.shard_map(local, mesh=mesh, in_specs=in_specs, out_specs=out_specs, check_vma=False)
```

profile of v0, /device:TPU:0, one launch (start us, length us, event | category | flops | bytes accessed | tf_op | source)
XLA Modules:
  0.0 78.4 jit_solution(11272599875550206099)
XLA Ops:
  0.6 1.2 %convert_element_type.52 = bf16[128,768]{1,0:T(8,128)(2,1)S(1)} convert(f32[128,768]{1,0:T(8,128)} %param.6) | non-fusion elementwise | flops 98304 | bytes 589824 | tf_op jit(solution)/shard_map/convert_element_type | solution.py:22
  2.5 5.4 %collective-permute-start.4 = (bf16[2,128,384]{2,1,0:T(8,128)(2,1)}, bf16[2,128,384]{2,1,0:T(8,128)(2,1)}, u32[]{:S(2)}, u32[]{:S(2)}) collective-permute-start(bf16[2,128,384]{2,1,0:T(8,128)(2,1)} %bitcast.80), channel_id=1, source_target_pairs={{1,0},{2,1},{3,2},{4,3},{5,4},{6,5},{7,6},{8,7},{9,8},{10,9},{11,1... | collective-permute-start | bytes 589832 | tf_op jit(solution)/shard_map/ppermute | solution.py:12
  10.6 3.5 %fusion.6 = bf16[10,128,384]{2,0,1:T(8,128)(2,1)S(1)} fusion(f32[2,128,5,384]{3,1,2,0:T(8,128)S(1)} %fusion.16, s32[2,5]{1,0:T(2,128)S(1)} %iota_add_fusion), kind=kOutput, calls=%fused_computation.10 | convolution fusion | flops 58982500 | bytes 2949160 | tf_op jit(solution)/shard_map/rkw,rkvb->wvb/dot_general | solution.py:28
  14.4 1.0 %copy-done.1 = bf16[10,128,384]{2,1,0:T(8,128)(2,1)} copy-done((bf16[10,128,384]{2,1,0:T(8,128)(2,1)}, bf16[10,128,384]{2,1,0:T(8,128)(2,1)S(1)}, u32[]{:S(2)}) %copy-start.1) | copy-done | bytes 983064
  17.9 0.9 %copy.18 = f32[128,768]{0,1:T(8,128)} copy(f32[128,768]{1,0:T(8,128)S(1)} %copy-done.5) | data formatting | bytes 786432 | tf_op args[1]
  18.8 1.9 %copy.14 = f32[128,768]{0,1:T(8,128)} copy(f32[128,768]{1,0:T(8,128)} %param.5) | data formatting | bytes 786432 | tf_op args[0]
  21.4 1.6 %constant_dynamic-update-slice_fusion.3 = bf16[10,128,384]{2,1,0:T(8,128)(2,1)} fusion(bf16[10,128,384]{2,1,0:T(8,128)(2,1)} %constant_dynamic-update-slice_fusion.4, bf16[2,128,384]{2,1,0:T(8,128)(2,1)} %collective-permute-done.4), kind=kLoop, calls=%fused_computation.33 | loop fusion | bytes 393216
  23.0 2.1 %collective-permute-start.2 = (bf16[2,128,384]{2,1,0:T(8,128)(2,1)}, bf16[2,128,384]{2,1,0:T(8,128)(2,1)S(1)}, u32[]{:S(2)}, u32[]{:S(2)}) collective-permute-start(bf16[2,128,384]{2,1,0:T(8,128)(2,1)} %get-tuple-element.12), channel_id=1, source_target_pairs={{13,0},{14,1},{15,2},{0,3},{1,4},{2,5},{3,6},{4,7},{5,8},{6,9},{7,... | collective-permute-start | bytes 589832 | tf_op jit(solution)/shard_map/ppermute | solution.py:12
  25.2 1.6 %constant_dynamic-update-slice_fusion.2 = bf16[10,128,384]{2,1,0:T(8,128)(2,1)} fusion(bf16[10,128,384]{2,1,0:T(8,128)(2,1)} %constant_dynamic-update-slice_fusion.3, bf16[2,128,384]{2,1,0:T(8,128)(2,1)} %collective-permute-done.5), kind=kLoop, calls=%fused_computation.32 | loop fusion | bytes 393216
  26.8 1.2 %collective-permute-start.3 = (bf16[2,128,384]{2,1,0:T(8,128)(2,1)}, bf16[2,128,384]{2,1,0:T(8,128)(2,1)S(1)}, u32[]{:S(2)}, u32[]{:S(2)}) collective-permute-start(bf16[2,128,384]{2,1,0:T(8,128)(2,1)} %get-tuple-element.11), channel_id=1, source_target_pairs={{12,0},{13,1},{14,2},{15,3},{0,4},{1,5},{2,6},{3,7},{4,8},{5,9},{6... | collective-permute-start | bytes 589832 | tf_op jit(solution)/shard_map/ppermute | solution.py:12
  27.9 1.6 %constant_dynamic-update-slice_fusion.1 = bf16[10,128,384]{2,1,0:T(8,128)(2,1)} fusion(bf16[10,128,384]{2,1,0:T(8,128)(2,1)} %constant_dynamic-update-slice_fusion.2, bf16[2,128,384]{2,1,0:T(8,128)(2,1)} %collective-permute-done.6), kind=kLoop, calls=%fused_computation.31 | loop fusion | bytes 393216
  29.6 1.6 %constant_dynamic-update-slice_fusion = bf16[10,128,384]{2,1,0:T(8,128)(2,1)} fusion(bf16[10,128,384]{2,1,0:T(8,128)(2,1)} %constant_dynamic-update-slice_fusion.1, bf16[2,128,384]{2,1,0:T(8,128)(2,1)} %collective-permute-done.7), kind=kLoop, calls=%fused_computation.30 | loop fusion | bytes 393216 | tf_op jit(solution)/shard_map/concatenate | solution.py:40
  31.2 2.0 %fusion.14 = bf16[2,5,128,384]{3,1,2,0:T(8,128)(2,1)S(1)} fusion(bf16[10,128,384,1]{2,1,0,3:T(8,128)(2,1)} %bitcast.90, s32[2,5]{1,0:T(2,128)S(1)} %iota_add_fusion), kind=kOutput, calls=%fused_computation.14 | convolution fusion | flops 9830500 | bytes 1966120 | tf_op jit(solution)/shard_map/rkw,wvb->rkvb/dot_general | solution.py:41
  33.3 1.0 %convolution_bitcast_fusion.1 = f32[2,128,384]{2,1,0:T(8,128)S(1)} fusion(bf16[2,5,384,384]{3,2,1,0:T(8,128)(2,1)S(1)} %bitcast.82, bf16[2,5,128,384]{3,1,2,0:T(8,128)(2,1)S(1)} %fusion.14), kind=kOutput, calls=%fused_computation.17 | convolution fusion | flops 377487360 | bytes 4325376 | tf_op jit(solution)/shard_map/rkab,rkvb->rva/dot_general | solution.py:47
  35.2 1.4 %multiply_bitcast_fusion.1 = f32[128,2,384]{2,0,1:T(8,128)S(1)} fusion(f32[2,128,384]{2,1,0:T(8,128)S(1)} %convolution_bitcast_fusion.1, bf16[2,128,384]{2,1,0:T(8,128)(2,1)S(1)} %collective-permute-done.3, bf16[2,128,384]{2,1,0:T(8,128)(2,1)S(1)} %collective-permute-done.2, bf16[2,128,384]{2,1,0:T(8,128)(2,1)S(1)} %collective-permute-done.1, ...), kind=kOutput, calls=%fused_computation.23 | convolution fusion | flops 76677120 | bytes 2555904 | tf_op jit(solution)/shard_map/rab,rvb->rva/dot_general | solution.py:31
  37.5 1.8 %fusion.31 = (bf16[128,768]{0,1:T(8,128)(2,1)}, f32[128,768]{0,1:T(8,128)S(1)}) fusion(f32[128,768]{0,1:T(8,128)} %copy.14, f32[128,2,384]{0,2,1:T(8,128)} %copy.13), kind=kLoop, calls=%fused_computation.49 | loop fusion | flops 196608 | bytes 1376256 | tf_op jit(solution)/shard_map/convert_element_type | solution.py:22
  39.4 1.1 %copy.15 = bf16[128,2,384]{2,0,1:T(8,128)(2,1)S(1)} copy(bf16[128,2,384]{0,2,1:T(8,128)(2,1)} %bitcast.95) | data formatting | bytes 393216 | tf_op jit(solution)/shard_map/reshape | solution.py:22
  41.2 2.9 %collective-permute-start.12 = (bf16[2,128,384]{2,1,0:T(8,128)(2,1)S(1)}, bf16[2,128,384]{2,1,0:T(8,128)(2,1)}, u32[]{:S(2)}, u32[]{:S(2)}) collective-permute-start(bf16[2,128,384]{2,1,0:T(8,128)(2,1)S(1)} %bitcast.91), channel_id=1, source_target_pairs={{1,0},{2,1},{3,2},{4,3},{5,4},{6,5},{7,6},{8,7},{9,8},{10,9},{11,1... | collective-permute-start | bytes 589832 | tf_op jit(solution)/shard_map/ppermute | solution.py:12
  44.9 2.1 %collective-permute-start.14 = (bf16[2,128,384]{2,1,0:T(8,128)(2,1)S(1)}, bf16[2,128,384]{2,1,0:T(8,128)(2,1)}, u32[]{:S(2)}, u32[]{:S(2)}) collective-permute-start(bf16[2,128,384]{2,1,0:T(8,128)(2,1)S(1)} %bitcast.93), channel_id=1, source_target_pairs={{3,0},{4,1},{5,2},{6,3},{7,4},{8,5},{9,6},{10,7},{11,8},{12,9},{13... | collective-permute-start | bytes 589832 | tf_op jit(solution)/shard_map/ppermute | solution.py:12
  48.6 3.5 %fusion.9 = bf16[10,128,384]{2,0,1:T(8,128)(2,1)S(1)} fusion(f32[2,128,5,384]{3,1,2,0:T(8,128)S(1)} %fusion.17, s32[2,5]{1,0:T(2,128)S(1)} %iota_add_fusion), kind=kOutput, calls=%fused_computation.11 | convolution fusion | flops 58982500 | bytes 2949160 | tf_op jit(solution)/shard_map/rkw,rkvb->wvb/dot_general | solution.py:28
  52.4 1.0 %copy-done.2 = bf16[10,128,384]{2,1,0:T(8,128)(2,1)} copy-done((bf16[10,128,384]{2,1,0:T(8,128)(2,1)}, bf16[10,128,384]{2,1,0:T(8,128)(2,1)S(1)}, u32[]{:S(2)}) %copy-start.2) | copy-done | bytes 983064
  56.3 1.6 %constant_dynamic-update-slice_fusion.8 = bf16[10,128,384]{2,1,0:T(8,128)(2,1)} fusion(bf16[10,128,384]{2,1,0:T(8,128)(2,1)} %constant_dynamic-update-slice_fusion.9, bf16[2,128,384]{2,1,0:T(8,128)(2,1)} %collective-permute-done.12), kind=kLoop, calls=%fused_computation.38 | loop fusion | bytes 393216
  58.1 1.6 %constant_dynamic-update-slice_fusion.7 = bf16[10,128,384]{2,1,0:T(8,128)(2,1)} fusion(bf16[10,128,384]{2,1,0:T(8,128)(2,1)} %constant_dynamic-update-slice_fusion.8, bf16[2,128,384]{2,1,0:T(8,128)(2,1)} %collective-permute-done.13), kind=kLoop, calls=%fused_computation.37 | loop fusion | bytes 393216
  59.8 1.9 %collective-permute-start.9 = (bf16[2,128,384]{2,1,0:T(8,128)(2,1)}, bf16[2,128,384]{2,1,0:T(8,128)(2,1)S(1)}, u32[]{:S(2)}, u32[]{:S(2)}) collective-permute-start(bf16[2,128,384]{2,1,0:T(8,128)(2,1)} %get-tuple-element.9), channel_id=1, source_target_pairs={{14,0},{15,1},{0,2},{1,3},{2,4},{3,5},{4,6},{5,7},{6,8},{7,9},{8,1... | collective-permute-start | bytes 589832 | tf_op jit(solution)/shard_map/ppermute | solution.py:12
  61.7 1.6 %constant_dynamic-update-slice_fusion.6 = bf16[10,128,384]{2,1,0:T(8,128)(2,1)} fusion(bf16[10,128,384]{2,1,0:T(8,128)(2,1)} %constant_dynamic-update-slice_fusion.7, bf16[2,128,384]{2,1,0:T(8,128)(2,1)} %collective-permute-done.14), kind=kLoop, calls=%fused_computation.36 | loop fusion | bytes 393216
  63.3 5.9 %collective-permute-done.15 = bf16[2,128,384]{2,1,0:T(8,128)(2,1)} collective-permute-done((bf16[2,128,384]{2,1,0:T(8,128)(2,1)S(1)}, bf16[2,128,384]{2,1,0:T(8,128)(2,1)}, u32[]{:S(2)}, u32[]{:S(2)}) %collective-permute-start.15) | collective-permute-done | bytes 196640 | tf_op jit(solution)/shard_map/ppermute | solution.py:12
  69.2 1.6 %constant_dynamic-update-slice_fusion.5 = bf16[10,128,384]{2,1,0:T(8,128)(2,1)} fusion(bf16[10,128,384]{2,1,0:T(8,128)(2,1)} %constant_dynamic-update-slice_fusion.6, bf16[2,128,384]{2,1,0:T(8,128)(2,1)} %collective-permute-done.15), kind=kLoop, calls=%fused_computation.35 | loop fusion | bytes 393216 | tf_op jit(solution)/shard_map/concatenate | solution.py:40
  70.8 2.0 %fusion.12 = bf16[2,5,128,384]{3,1,2,0:T(8,128)(2,1)S(1)} fusion(bf16[10,128,384,1]{2,1,0,3:T(8,128)(2,1)} %bitcast.89, s32[2,5]{1,0:T(2,128)S(1)} %iota_add_fusion), kind=kOutput, calls=%fused_computation.12 | convolution fusion | flops 9830500 | bytes 1966120 | tf_op jit(solution)/shard_map/rkw,wvb->rkvb/dot_general | solution.py:41
  72.9 1.0 %convolution_bitcast_fusion = f32[2,128,384]{2,1,0:T(8,128)S(1)} fusion(bf16[2,5,384,384]{3,2,1,0:T(8,128)(2,1)S(1)} %bitcast.84, bf16[2,5,128,384]{3,1,2,0:T(8,128)(2,1)S(1)} %fusion.12), kind=kOutput, calls=%fused_computation.16 | convolution fusion | flops 377487360 | bytes 4325376 | tf_op jit(solution)/shard_map/rkab,rkvb->rva/dot_general | solution.py:47
  73.9 1.4 %multiply_bitcast_fusion = f32[128,2,384]{2,0,1:T(8,128)S(1)} fusion(f32[2,128,384]{2,1,0:T(8,128)S(1)} %convolution_bitcast_fusion, bf16[2,128,384]{2,1,0:T(8,128)(2,1)S(1)} %collective-permute-done.11, bf16[2,128,384]{2,1,0:T(8,128)(2,1)} %collective-permute-done.10, bf16[2,128,384]{2,1,0:T(8,128)(2,1)S(1)} %collective-permute-done.9, ...), kind=kOutput, calls=%fused_computation.22 | convolution fusion | flops 76677120 | bytes 2555904 | tf_op jit(solution)/shard_map/rab,rvb->rva/dot_general | solution.py:31
  76.3 1.2 %bitcast_subtract_fusion = f32[128,768]{0,1:T(8,128)S(1)} fusion(f32[128,768]{0,1:T(8,128)} %copy.18, f32[128,2,384]{0,2,1:T(8,128)} %copy.17), kind=kLoop, calls=%fused_computation.20 | loop fusion | flops 98304 | bytes 1179648 | tf_op jit(solution)/shard_map/sub | solution.py:55
  77.4 0.9 %copy.20 = f32[128,768]{1,0:T(8,128)} copy(f32[128,768]{0,1:T(8,128)S(1)} %bitcast_subtract_fusion) | data formatting | bytes 786432
  (48 shorter events, 16.1 us)
Async XLA Ops:
  0.6 9.3 %copy-start = (bf16[10,384,384]{2,1,0:T(8,128)(2,1)S(1)}, bf16[10,384,384]{2,1,0:T(8,128)(2,1)}, u32[]{:S(2)}) copy-start(bf16[10,384,384]{2,1,0:T(8,128)(2,1)} %param.8) | copy-start | bytes 8847364
  2.5 18.2 %collective-permute-start.4 = (bf16[2,128,384]{2,1,0:T(8,128)(2,1)}, bf16[2,128,384]{2,1,0:T(8,128)(2,1)}, u32[]{:S(2)}, u32[]{:S(2)}) collective-permute-start(bf16[2,128,384]{2,1,0:T(8,128)(2,1)} %bitcast.80), channel_id=1, source_target_pairs={{1,0},{2,1},{3,2},{4,3},{5,4},{6,5},{7,6},{8,7},{9,8},{10,9},{11,1... | collective-permute-start | bytes 589832 | tf_op jit(solution)/shard_map/ppermute | solution.py:12
  7.9 15.1 %collective-permute-start.5 = (bf16[2,128,384]{2,1,0:T(8,128)(2,1)}, bf16[2,128,384]{2,1,0:T(8,128)(2,1)}, u32[]{:S(2)}, u32[]{:S(2)}) collective-permute-start(bf16[2,128,384]{2,1,0:T(8,128)(2,1)} %bitcast.80), channel_id=1, source_target_pairs={{2,0},{3,1},{4,2},{5,3},{6,4},{7,5},{8,6},{9,7},{10,8},{11,9},{12,... | collective-permute-start | bytes 589832 | tf_op jit(solution)/shard_map/ppermute | solution.py:12
  8.5 18.3 %collective-permute-start.6 = (bf16[2,128,384]{2,1,0:T(8,128)(2,1)}, bf16[2,128,384]{2,1,0:T(8,128)(2,1)}, u32[]{:S(2)}, u32[]{:S(2)}) collective-permute-start(bf16[2,128,384]{2,1,0:T(8,128)(2,1)} %bitcast.80), channel_id=1, source_target_pairs={{3,0},{4,1},{5,2},{6,3},{7,4},{8,5},{9,6},{10,7},{11,8},{12,9},{13... | collective-permute-start | bytes 589832 | tf_op jit(solution)/shard_map/ppermute | solution.py:12
  8.8 20.8 %collective-permute-start.7 = (bf16[2,128,384]{2,1,0:T(8,128)(2,1)}, bf16[2,128,384]{2,1,0:T(8,128)(2,1)}, u32[]{:S(2)}, u32[]{:S(2)}) collective-permute-start(bf16[2,128,384]{2,1,0:T(8,128)(2,1)} %bitcast.80), channel_id=1, source_target_pairs={{4,0},{5,1},{6,2},{7,3},{8,4},{9,5},{10,6},{11,7},{12,8},{13,9},{1... | collective-permute-start | bytes 589832 | tf_op jit(solution)/shard_map/ppermute | solution.py:12
  14.2 3.7 %copy-start.5 = (f32[128,768]{1,0:T(8,128)S(1)}, f32[128,768]{1,0:T(8,128)}, u32[]{:S(2)}) copy-start(f32[128,768]{1,0:T(8,128)} %param.6) | copy-start | bytes 1179652
  14.4 1.0 %copy-start.1 = (bf16[10,128,384]{2,1,0:T(8,128)(2,1)}, bf16[10,128,384]{2,1,0:T(8,128)(2,1)S(1)}, u32[]{:S(2)}) copy-start(bf16[10,128,384]{2,1,0:T(8,128)(2,1)S(1)} %copy.66) | copy-start | bytes 2949124
  16.3 18.0 %collective-permute-start = (bf16[2,128,384]{2,1,0:T(8,128)(2,1)}, bf16[2,128,384]{2,1,0:T(8,128)(2,1)}, u32[]{:S(2)}, u32[]{:S(2)}) collective-permute-start(bf16[2,128,384]{2,1,0:T(8,128)(2,1)} %get-tuple-element.10), channel_id=1, source_target_pairs={{15,0},{0,1},{1,2},{2,3},{3,4},{4,5},{5,6},{6,7},{7,8},{8,9},{9,10... | collective-permute-start | bytes 589832 | tf_op jit(solution)/shard_map/ppermute | solution.py:12
  20.7 13.6 %collective-permute-start.1 = (bf16[2,128,384]{2,1,0:T(8,128)(2,1)}, bf16[2,128,384]{2,1,0:T(8,128)(2,1)S(1)}, u32[]{:S(2)}, u32[]{:S(2)}) collective-permute-start(bf16[2,128,384]{2,1,0:T(8,128)(2,1)} %get-tuple-element.13), channel_id=1, source_target_pairs={{14,0},{15,1},{0,2},{1,3},{2,4},{3,5},{4,6},{5,7},{6,8},{7,9},{8,1... | collective-permute-start | bytes 589832 | tf_op jit(solution)/shard_map/ppermute | solution.py:12
  23.0 11.2 %collective-permute-start.2 = (bf16[2,128,384]{2,1,0:T(8,128)(2,1)}, bf16[2,128,384]{2,1,0:T(8,128)(2,1)S(1)}, u32[]{:S(2)}, u32[]{:S(2)}) collective-permute-start(bf16[2,128,384]{2,1,0:T(8,128)(2,1)} %get-tuple-element.12), channel_id=1, source_target_pairs={{13,0},{14,1},{15,2},{0,3},{1,4},{2,5},{3,6},{4,7},{5,8},{6,9},{7,... | collective-permute-start | bytes 589832 | tf_op jit(solution)/shard_map/ppermute | solution.py:12
  26.8 8.4 %collective-permute-start.3 = (bf16[2,128,384]{2,1,0:T(8,128)(2,1)}, bf16[2,128,384]{2,1,0:T(8,128)(2,1)S(1)}, u32[]{:S(2)}, u32[]{:S(2)}) collective-permute-start(bf16[2,128,384]{2,1,0:T(8,128)(2,1)} %get-tuple-element.11), channel_id=1, source_target_pairs={{12,0},{13,1},{14,2},{15,3},{0,4},{1,5},{2,6},{3,7},{4,8},{5,9},{6... | collective-permute-start | bytes 589832 | tf_op jit(solution)/shard_map/ppermute | solution.py:12
  33.3 1.9 %copy-start.3 = (bf16[2,384,384]{2,1,0:T(8,128)(2,1)S(1)}, bf16[2,384,384]{2,1,0:T(8,128)(2,1)}, u32[]{:S(2)}) copy-start(bf16[2,384,384]{2,1,0:T(8,128)(2,1)} %param.7) | copy-start | bytes 1769476
  41.2 14.7 %collective-permute-start.12 = (bf16[2,128,384]{2,1,0:T(8,128)(2,1)S(1)}, bf16[2,128,384]{2,1,0:T(8,128)(2,1)}, u32[]{:S(2)}, u32[]{:S(2)}) collective-permute-start(bf16[2,128,384]{2,1,0:T(8,128)(2,1)S(1)} %bitcast.91), channel_id=1, source_target_pairs={{1,0},{2,1},{3,2},{4,3},{5,4},{6,5},{7,6},{8,7},{9,8},{10,9},{11,1... | collective-permute-start | bytes 589832 | tf_op jit(solution)/shard_map/ppermute | solution.py:12
  44.1 13.9 %collective-permute-start.13 = (bf16[2,128,384]{2,1,0:T(8,128)(2,1)S(1)}, bf16[2,128,384]{2,1,0:T(8,128)(2,1)}, u32[]{:S(2)}, u32[]{:S(2)}) collective-permute-start(bf16[2,128,384]{2,1,0:T(8,128)(2,1)S(1)} %bitcast.92), channel_id=1, source_target_pairs={{2,0},{3,1},{4,2},{5,3},{6,4},{7,5},{8,6},{9,7},{10,8},{11,9},{12,... | collective-permute-start | bytes 589832 | tf_op jit(solution)/shard_map/ppermute | solution.py:12
  44.9 14.8 %collective-permute-start.14 = (bf16[2,128,384]{2,1,0:T(8,128)(2,1)S(1)}, bf16[2,128,384]{2,1,0:T(8,128)(2,1)}, u32[]{:S(2)}, u32[]{:S(2)}) collective-permute-start(bf16[2,128,384]{2,1,0:T(8,128)(2,1)S(1)} %bitcast.93), channel_id=1, source_target_pairs={{3,0},{4,1},{5,2},{6,3},{7,4},{8,5},{9,6},{10,7},{11,8},{12,9},{13... | collective-permute-start | bytes 589832 | tf_op jit(solution)/shard_map/ppermute | solution.py:12
  47.0 22.2 %collective-permute-start.15 = (bf16[2,128,384]{2,1,0:T(8,128)(2,1)S(1)}, bf16[2,128,384]{2,1,0:T(8,128)(2,1)}, u32[]{:S(2)}, u32[]{:S(2)}) collective-permute-start(bf16[2,128,384]{2,1,0:T(8,128)(2,1)S(1)} %bitcast.94), channel_id=1, source_target_pairs={{4,0},{5,1},{6,2},{7,3},{8,4},{9,5},{10,6},{11,7},{12,8},{13,9},{1... | collective-permute-start | bytes 589832 | tf_op jit(solution)/shard_map/ppermute | solution.py:12
  52.3 1.0 %copy-start.2 = (bf16[10,128,384]{2,1,0:T(8,128)(2,1)}, bf16[10,128,384]{2,1,0:T(8,128)(2,1)S(1)}, u32[]{:S(2)}) copy-start(bf16[10,128,384]{2,1,0:T(8,128)(2,1)S(1)} %copy.65) | copy-start | bytes 2949124
  54.2 19.7 %collective-permute-start.10 = (bf16[2,128,384]{2,1,0:T(8,128)(2,1)}, bf16[2,128,384]{2,1,0:T(8,128)(2,1)}, u32[]{:S(2)}, u32[]{:S(2)}) collective-permute-start(bf16[2,128,384]{2,1,0:T(8,128)(2,1)} %get-tuple-element.8), channel_id=1, source_target_pairs={{13,0},{14,1},{15,2},{0,3},{1,4},{2,5},{3,6},{4,7},{5,8},{6,9},{7,... | collective-permute-start | bytes 589832 | tf_op jit(solution)/shard_map/ppermute | solution.py:12
  55.9 18.0 %collective-permute-start.11 = (bf16[2,128,384]{2,1,0:T(8,128)(2,1)}, bf16[2,128,384]{2,1,0:T(8,128)(2,1)S(1)}, u32[]{:S(2)}, u32[]{:S(2)}) collective-permute-start(bf16[2,128,384]{2,1,0:T(8,128)(2,1)} %get-tuple-element.7), channel_id=1, source_target_pairs={{12,0},{13,1},{14,2},{15,3},{0,4},{1,5},{2,6},{3,7},{4,8},{5,9},{6... | collective-permute-start | bytes 589832 | tf_op jit(solution)/shard_map/ppermute | solution.py:12
  58.0 15.9 %collective-permute-start.8 = (bf16[2,128,384]{2,1,0:T(8,128)(2,1)}, bf16[2,128,384]{2,1,0:T(8,128)(2,1)S(1)}, u32[]{:S(2)}, u32[]{:S(2)}) collective-permute-start(bf16[2,128,384]{2,1,0:T(8,128)(2,1)} %get-tuple-element.6), channel_id=1, source_target_pairs={{15,0},{0,1},{1,2},{2,3},{3,4},{4,5},{5,6},{6,7},{7,8},{8,9},{9,10... | collective-permute-start | bytes 589832 | tf_op jit(solution)/shard_map/ppermute | solution.py:12
  59.8 14.1 %collective-permute-start.9 = (bf16[2,128,384]{2,1,0:T(8,128)(2,1)}, bf16[2,128,384]{2,1,0:T(8,128)(2,1)S(1)}, u32[]{:S(2)}, u32[]{:S(2)}) collective-permute-start(bf16[2,128,384]{2,1,0:T(8,128)(2,1)} %get-tuple-element.9), channel_id=1, source_target_pairs={{14,0},{15,1},{0,2},{1,3},{2,4},{3,5},{4,6},{5,7},{6,8},{7,9},{8,1... | collective-permute-start | bytes 589832 | tf_op jit(solution)/shard_map/ppermute | solution.py:12
  72.9 1.1 %copy-start.4 = (bf16[2,384,384]{2,1,0:T(8,128)(2,1)S(1)}, bf16[2,384,384]{2,1,0:T(8,128)(2,1)}, u32[]{:S(2)}) copy-start(bf16[2,384,384]{2,1,0:T(8,128)(2,1)} %param.7) | copy-start | bytes 1769476
where the time goes:
time: 79 us; the launch traced here: 78.4 us
  local copies, waits for them, and re-layouts  26.9 us (34%)
  starting transfers between devices  21.5 us (27%)
  matrix products  17.4 us (22%)
  waiting for transfers between devices  6.78 us (9%)
  other arithmetic  4.85 us (6%)
  between operations  0.84 us (1%)
    ppermute x16, starting transfers between devices, passed_along(): return lax.ppermute(block, axis, route)  21.5 us
    unnamed x24, local copies, waits for them, and re-layouts  17.8 us
    dot_general x2, matrix products, apply_operator(): jnp.einsum('rkw,rkvb->wvb', selector.astype(jnp.float32), transposed, pre...  7.08 us
    ppermute x16, waiting for transfers between devices, passed_along(): return lax.ppermute(block, axis, route)  6.78 us
    dot_general x2, matrix products, apply_operator(): jnp.einsum('rkw,wvb->rkvb', selector.astype(jnp.bfloat16), neighbor_block...  4.07 us
    concatenate x2, local copies, waits for them, and re-layouts, apply_operator(): neighbor_blocks = jnp.concatenate(groups, axis=0)  3.27 us
    convert_element_type x2, other arithmetic, apply_operator(): current.astype(jnp.bfloat16).reshape(vectors, blocks_of_row, block_size)  3.02 us
    dot_general x2, matrix products, apply_operator(): jnp.einsum('rab,rvb->rva', diag_blocks, sendable, preferred_element_type=...  2.86 us
  transfers between devices with their start and end apart: 16, of which 2 were waited for; matrix products, arithmetic and copies ran while one was open for 45% of the time, Pallas kernels for 0%

commit v1 on v0

v1 whole, which is shorter than its diff:
```python
import functools

import jax
import jax.numpy as jnp
from jax import lax
from jax.experimental import pallas as pl
from jax.experimental.pallas import tpu as pltpu
from jax.sharding import PartitionSpec as P

HOPS = 4
CHUNKS = 2
AXES = ("grp", "atoms", "vec", "sub")
MESH = pl.DeviceIdType.MESH
F32 = jnp.float32
BF16 = jnp.bfloat16

FAR, NEAR, MATE_NEAR, MATE_FAR, PART_NEAR, PART_FAR, PART_X, PART_Z = range(8)


def kernel(
    n_atoms, n_vec, offsets, t_cur, t_prev_hbm, diag_hbm, stored_hbm, t_one, t_two,
    diag, stored, t_prev, products, sums, own, *rest,
):
    steps = 2 * CHUNKS
    windows, outgoing, incoming = rest[:steps], rest[steps:2 * steps], rest[2 * steps:3 * steps]
    load_sem, send_sem, recv_sem = rest[3 * steps:]
    size = diag.shape[1]
    slots = offsets.shape[1]
    rows = t_cur.shape[0] // CHUNKS
    tree = n_vec == 2

    g, z, x, c = [lax.axis_index(name) for name in AXES]
    chips = n_atoms * n_vec
    place = z * n_vec + x

    def chip(step):
        at = lax.rem(place + step + chips, chips)
        return (g, at // n_vec, lax.rem(at, n_vec), c)

    mate = (g, z, x, 1 - c)
    far_ahead, far_behind = chip(2), chip(-2)
    if tree:
        near_ahead = near_behind = (g, z, 1 - x, c)
        partners = (mate, near_ahead, far_ahead, far_behind)
    else:
        near_ahead, near_behind = chip(1), chip(-1)
        partners = (mate, near_ahead, near_behind, far_ahead, far_behind)

    loads = [
        pltpu.make_async_copy(stored_hbm, stored, load_sem.at[0]),
        pltpu.make_async_copy(diag_hbm, diag, load_sem.at[1]),
        pltpu.make_async_copy(t_prev_hbm, t_prev, load_sem.at[2]),
    ]
    for load in loads:
        load.start()

    barrier = pltpu.get_barrier_semaphore()
    for partner in partners:
        pl.semaphore_signal(barrier, inc=1, device_id=partner, device_id_type=MESH)

    named = [[offsets[r, k] for k in range(slots)] for r in range(2)]
    found = []
    for r in range(2):
        of_row = {}
        for offset in range(1, 2 * HOPS + 1):
            at = jnp.int32(slots)
            for k in range(slots):
                at = jnp.where(named[r][k] == offset, jnp.int32(k), at)
            of_row[offset] = at
        found.append(of_row)
    for r in range(2):
        products[r, slots] = jnp.zeros((rows, size), F32)

    def copies(s):
        window, out, arrive = windows[s], outgoing[s], incoming[s]

        def copy(which, src, dst, device):
            return pltpu.make_async_remote_copy(
                src_ref=src, dst_ref=dst, send_sem=send_sem.at[s, which],
                recv_sem=recv_sem.at[s, which], device_id=device, device_id_type=MESH,
            )

        near_src = 8 * (1 - x) if tree else 0
        return {
            FAR: copy(FAR, window.at[pl.ds(0, 2)], window.at[pl.ds(8, 2)], far_behind),
            NEAR: copy(NEAR, window.at[pl.ds(near_src, 2)], window.at[pl.ds(4, 2)], near_behind),
            MATE_NEAR: copy(MATE_NEAR, window.at[pl.ds(4, 2)], window.at[pl.ds(2 + 4 * c, 2)], mate),
            MATE_FAR: copy(
                MATE_FAR, window.at[pl.ds(8 * (1 - c), 2)], window.at[pl.ds(6 - 4 * c, 2)], mate
            ),
            PART_NEAR: copy(PART_NEAR, out.at[0], arrive.at[0], mate),
            PART_FAR: copy(PART_FAR, out.at[1], arrive.at[1], mate),
            PART_X: copy(PART_X, out.at[2], arrive.at[2], near_ahead),
            PART_Z: copy(PART_Z, out.at[3], arrive.at[3], far_ahead),
        }

    every = [copies(s) for s in range(steps)]

    def send_vectors(s, value):
        windows[s][0] = value[:, :size].astype(BF16)
        windows[s][1] = value[:, size:].astype(BF16)
        every[s][FAR].start()
        if tree:
            @pl.when(x == 1)
            def _():
                every[s][NEAR].start()
        else:
            every[s][NEAR].start()

    def compute_parts(s):
        window, out = windows[s], outgoing[s]
        for r in range(2):
            block = window[r]
            for k in range(slots):
                products[r, k] = jnp.dot(block, stored[r * slots + k], preferred_element_type=F32)

        def part(w):
            total = None
            if 1 <= w <= 2 * HOPS:
                total = products[0, found[0][w]]
            if 1 <= w - 1 <= 2 * HOPS:
                term = products[1, found[1][w - 1]]
                total = term if total is None else total + term
            return total

        near = jnp.where(c == 0, 0, 1)
        for i in range(2):
            one, three = part(2 + i), part(6 + i)
            out[near, i] = three.astype(BF16)
            out[1 - near, i] = one.astype(BF16)
        every[s][PART_NEAR].start()
        every[s][PART_FAR].start()
        for i in range(2):
            sums[s, i] = part(4 + i)
            sums[s, 2 + i] = part(8 + i)
        sums[s, 4] = part(1)

    def join_parts(s):
        out, arrive = outgoing[s], incoming[s]
        every[s][PART_NEAR].wait_recv()
        for i in range(2):
            out[2, i] = (sums[s, i] + arrive[0, i].astype(F32)).astype(BF16)
        every[s][PART_X].start()
        every[s][PART_FAR].wait_recv()
        for i in range(2):
            extra = arrive[1, i].astype(F32)
            sums[s, 2 + i] = sums[s, 2 + i] + jnp.where(c == 0, extra, 0.0)
            extra = jnp.where(c == 1, extra, 0.0)
            own[s, i] = extra + sums[s, 4] if i == 1 else extra
        if tree:
            @pl.when(x == 1)
            def _():
                send_far_part(s, False)
        else:
            send_far_part(s, False)

    def send_far_part(s, add):
        out, arrive = outgoing[s], incoming[s]
        for i in range(2):
            total = sums[s, 2 + i]
            if add:
                total = total + arrive[2, i].astype(F32)
            out[3, i] = total.astype(BF16)
        every[s][PART_Z].start()

    def relay_vectors(s):
        every[s][FAR].wait_recv()
        every[s][MATE_FAR].start()
        if tree:
            @pl.when(x == 0)
            def _():
                every[s][NEAR].start()

    def relay_parts(s):
        if tree:
            @pl.when(x == 0)
            def _():
                every[s][PART_X].wait_recv()
                send_far_part(s, True)

    def spread_vectors(s):
        every[s][NEAR].wait_recv()
        every[s][MATE_NEAR].start()

    def multiply(s):
        every[s][MATE_NEAR].wait_recv()
        every[s][MATE_FAR].wait_recv()
        window = windows[s]
        for r in range(2):
            total = jnp.dot(window[r], diag[r], preferred_element_type=F32)
            for k in range(slots):
                total = total + lax.dot_general(
                    window[r + named[r][k]], stored[r * slots + k],
                    (((1,), (1,)), ((), ())), preferred_element_type=F32,
                )
            own[s, r] = own[s, r] + total

    def finish(s, before, result, part_rows):
        arrive = incoming[s]
        if tree:
            @pl.when(x == 1)
            def _():
                every[s][PART_X].wait_recv()
        else:
            every[s][PART_X].wait_recv()
        every[s][PART_Z].wait_recv()
        for r in range(2):
            total = own[s, r] + arrive[3, r].astype(F32)
            near = arrive[2, r].astype(F32)
            total = total + (jnp.where(x == 1, near, 0.0) if tree else near)
            cols = pl.ds(r * size, size)
            result[part_rows, cols] = 2.0 * total - before[part_rows, cols]

    chunk_rows = [pl.ds(h * rows, rows) for h in range(CHUNKS)]
    first = list(range(CHUNKS))
    second = [CHUNKS + h for h in first]

    pl.semaphore_wait(barrier, len(partners))
    for h in first:
        send_vectors(h, t_cur[chunk_rows[h], :])
    loads[0].wait()
    for h in first:
        compute_parts(h)
    for h in first:
        join_parts(h)
    loads[1].wait()
    loads[2].wait()
    for h in first:
        relay_vectors(h)
        relay_parts(h)
    for h in first:
        spread_vectors(h)
    for h in first:
        multiply(h)
        finish(h, t_prev, t_one, chunk_rows[h])
        s = second[h]
        send_vectors(s, t_one[chunk_rows[h], :])
        compute_parts(s)
        join_parts(s)
    for h in first:
        relay_vectors(second[h])
        relay_parts(second[h])
    for h in first:
        spread_vectors(second[h])
    for h in first:
        multiply(second[h])
        finish(second[h], t_cur, t_two, chunk_rows[h])
    for s in range(steps):
        for copy in every[s].values():
            copy.wait_send()


def solution(mesh):
    n_atoms, n_vec = mesh.shape["atoms"], mesh.shape["vec"]

    def local(t_prev, t_cur, diag_blocks, upper_half_blocks, offsets):
        rows = t_cur.shape[0] // CHUNKS
        size = diag_blocks.shape[1]
        slots = offsets.shape[1]
        steps = 2 * CHUNKS
        vmem = pl.BlockSpec(memory_space=pltpu.VMEM)
        hbm = pl.BlockSpec(memory_space=pl.ANY)
        return pl.pallas_call(
            functools.partial(kernel, n_atoms, n_vec),
            out_shape=(
                jax.ShapeDtypeStruct(t_cur.shape, F32), jax.ShapeDtypeStruct(t_cur.shape, F32)
            ),
            in_specs=[pl.BlockSpec(memory_space=pltpu.SMEM), vmem, hbm, hbm, hbm],
            out_specs=(vmem, vmem),
            scratch_shapes=[
                pltpu.VMEM(diag_blocks.shape, BF16),
                pltpu.VMEM(upper_half_blocks.shape, BF16),
                pltpu.VMEM(t_prev.shape, F32),
                pltpu.VMEM((2, slots + 1, rows, size), F32),
                pltpu.VMEM((steps, 5, rows, size), F32),
                pltpu.VMEM((steps, 2, rows, size), F32),
                *[pltpu.VMEM((2 * HOPS + 2, rows, size), BF16) for _ in range(steps)],
                *[pltpu.VMEM((4, 2, rows, size), BF16) for _ in range(2 * steps)],
                pltpu.SemaphoreType.DMA((3,)),
                pltpu.SemaphoreType.DMA((steps, 8)),
                pltpu.SemaphoreType.DMA((steps, 8)),
            ],
            compiler_params=pltpu.CompilerParams(
                collective_id=0, has_side_effects=True, vmem_limit_bytes=48 << 20
            ),
        )(offsets, t_cur, t_prev, diag_blocks, upper_half_blocks)

    in_specs = (
        P("grp", ("atoms", "vec", "sub")),
        P("grp", ("atoms", "vec", "sub")),
        P(AXES, None, None),
        P(AXES, None, None),
        P(AXES, None),
    )
    out_specs = (P("grp", ("atoms", "vec", "sub")), P("grp", ("atoms", "vec", "sub")))
    return jax.shard_map(local, mesh=mesh, in_specs=in_specs, out_specs=out_specs, check_vma=False)
```

time: 79 us -> 43.1 us (0.55)
  Pallas kernels: 0 us -> 35.1 us
  starting transfers between devices: 21.5 us -> 0 us
  local copies, waits for them, and re-layouts: 26.9 us -> 7.05 us
  matrix products: 17.4 us -> 0 us
  waiting for transfers between devices: 6.78 us -> 0 us
  other arithmetic: 4.85 us -> 0 us
    pallas_call x0 -> x1, Pallas kernels: none -> 35.1 us  [local(): pl.pallas_call(functools.partial(kernel, n_atoms, n_vec), out_shape=(jax....]
    ppermute x16 -> x0, starting transfers between devices: 21.5 us -> none  [passed_along(): return lax.ppermute(block, axis, route)]
    dot_general x10 -> x0, matrix products: 17.4 us -> none  [the longest x2 7.08 us: apply_operator(): jnp.einsum('rkw,rkvb->wvb', selector.astype(jnp.float32), transposed, pre...]
    unnamed x24 -> x12, local copies, waits for them, and re-layouts: 17.8 us -> 7.05 us
    ppermute x16 -> x0, waiting for transfers between devices: 6.78 us -> none  [passed_along(): return lax.ppermute(block, axis, route)]
    concatenate x2 -> x0, local copies, waits for them, and re-layouts: 3.27 us -> none  [apply_operator(): neighbor_blocks = jnp.concatenate(groups, axis=0)]
    convert_element_type x2 -> x0, other arithmetic: 3.02 us -> none  [apply_operator(): current.astype(jnp.bfloat16).reshape(vectors, blocks_of_row, block_size)]
    mul x2 -> x0, local copies, waits for them, and re-layouts: 1.83 us -> none  [the longest x1 0.91 us: local(): 2.0 * apply_operator(t_cur, diag_blocks, upper_half_blocks, offsets)]
  transfers between devices with their start and end apart: 16 -> 0, of which waited for: 2 -> 0; matrix products, arithmetic and copies ran while one was open for 45% -> 0% of each run, Pallas kernels for 0% -> 0%
where the time goes in v1:
time: 43.1 us; the launch traced here: 42.8 us
  Pallas kernels  35.1 us (81%)
  local copies, waits for them, and re-layouts  7.05 us (16%)
  between operations  0.65 us (2%)
    pallas_call x1, Pallas kernels, local(): pl.pallas_call(functools.partial(kernel, n_atoms, n_vec), out_shape=(jax....  35.1 us
    unnamed x12, local copies, waits for them, and re-layouts  7.05 us

profile of v1, /device:TPU:0, one launch (start us, length us, event | category | flops | bytes accessed | tf_op | source)
XLA Modules:
  0.0 42.8 jit_solution(8354093780790968136)
XLA Ops:
  0.6 0.0 copy-start
  0.6 1.8 %copy-done = bf16[10,384,384]{2,1,0:T(8,128)(2,1)S(1)} copy-done((bf16[10,384,384]{2,1,0:T(8,128)(2,1)S(1)}, bf16[10,384,384]{2,1,0:T(8,128)(2,1)}, u32[]{:S(2)}) %copy-start) | copy-done | bytes 2949144
  2.5 0.0 copy-start.1
  2.5 1.1 %copy-done.1 = bf16[2,384,384]{2,1,0:T(8,128)(2,1)S(1)} copy-done((bf16[2,384,384]{2,1,0:T(8,128)(2,1)S(1)}, bf16[2,384,384]{2,1,0:T(8,128)(2,1)}, u32[]{:S(2)}) %copy-start.1) | copy-done | bytes 589848
  3.5 0.0 copy-start.2
  3.5 1.0 %copy-done.2 = f32[128,768]{1,0:T(8,128)S(1)} copy-done((f32[128,768]{1,0:T(8,128)S(1)}, f32[128,768]{1,0:T(8,128)}, u32[]{:S(2)}) %copy-start.2) | copy-done | bytes 393240
  4.5 0.0 copy-start.3
  4.5 1.0 %copy-done.3 = f32[128,768]{1,0:T(8,128)S(1)} copy-done((f32[128,768]{1,0:T(8,128)S(1)}, f32[128,768]{1,0:T(8,128)}, u32[]{:S(2)}) %copy-start.3) | copy-done | bytes 393240
  5.5 0.0 copy-start.4
  5.5 0.7 %copy-done.4 = s32[2,5]{1,0:T(2,128)S(1)} copy-done((s32[2,5]{1,0:T(2,128)S(1)}, s32[2,5]{1,0:T(2,128)}, u32[]{:S(2)}) %copy-start.4) | copy-done | bytes 64
  6.2 35.1 %shard_map.68 = (f32[128,768]{1,0:T(8,128)S(1)}, f32[128,768]{1,0:T(8,128)S(1)}) custom-call(s32[2,5]{1,0:T(2,128)S(1)} %copy-done.4, f32[128,768]{1,0:T(8,128)S(1)} %copy-done.2, f32[128,768]{1,0:T(8,128)S(1)} %copy-done.3, bf16[2,384,384]{2,1,0:T(8,128)(2,1)S(1)} %copy-done.1, bf16[10,384,384]{2,1,0:T(8,128)(2,1)S(1)} %copy-done), custom_call_target="tpu_custom_call" | custom-call | tf_op jit(solution)/shard_map/pallas_call | solution.py:263
  41.3 0.7 %copy.9 = f32[128,768]{1,0:T(8,128)} copy(f32[128,768]{1,0:T(8,128)S(1)} %get-tuple-element.4) | data formatting | bytes 786432
  42.0 0.7 %copy.10 = f32[128,768]{1,0:T(8,128)} copy(f32[128,768]{1,0:T(8,128)S(1)} %get-tuple-element.5) | data formatting | bytes 786432
Async XLA Ops:
  0.6 1.8 %copy-start = (bf16[10,384,384]{2,1,0:T(8,128)(2,1)S(1)}, bf16[10,384,384]{2,1,0:T(8,128)(2,1)}, u32[]{:S(2)}) copy-start(bf16[10,384,384]{2,1,0:T(8,128)(2,1)} %stored_hbm.1) | copy-start | bytes 8847364
  2.5 1.1 %copy-start.1 = (bf16[2,384,384]{2,1,0:T(8,128)(2,1)S(1)}, bf16[2,384,384]{2,1,0:T(8,128)(2,1)}, u32[]{:S(2)}) copy-start(bf16[2,384,384]{2,1,0:T(8,128)(2,1)} %diag_hbm.1) | copy-start | bytes 1769476
  3.5 1.0 %copy-start.2 = (f32[128,768]{1,0:T(8,128)S(1)}, f32[128,768]{1,0:T(8,128)}, u32[]{:S(2)}) copy-start(f32[128,768]{1,0:T(8,128)} %t_cur.1) | copy-start | bytes 1179652
  4.5 1.0 %copy-start.3 = (f32[128,768]{1,0:T(8,128)S(1)}, f32[128,768]{1,0:T(8,128)}, u32[]{:S(2)}) copy-start(f32[128,768]{1,0:T(8,128)} %t_prev_hbm.1) | copy-start | bytes 1179652
  5.5 0.7 %copy-start.4 = (s32[2,5]{1,0:T(2,128)S(1)}, s32[2,5]{1,0:T(2,128)}, u32[]{:S(2)}) copy-start(s32[2,5]{1,0:T(2,128)} %offsets.1) | copy-start | bytes 124

commit v2 on v1

v2 whole, which is shorter than its diff:
```python
import functools

import jax
import jax.numpy as jnp
from jax import lax
from jax.experimental import pallas as pl
from jax.experimental.pallas import tpu as pltpu
from jax.sharding import PartitionSpec as P

HOPS = 4
CHUNKS = 2
PIECES = 2
AXES = ("grp", "atoms", "vec", "sub")
MESH = pl.DeviceIdType.MESH
F32 = jnp.float32
BF16 = jnp.bfloat16

FAR, NEAR, MATE_NEAR, MATE_FAR, PART_NEAR, PART_FAR, PART_X, PART_Z = range(8)


def kernel(
    n_atoms, n_vec, offsets_hbm, t_cur_hbm, t_prev_hbm, diag_hbm, stored_hbm, t_one, t_two,
    offsets, t_cur, t_prev, diag, stored, sums, own, *rest,
):
    steps = 2 * CHUNKS
    windows, outgoing, incoming = rest[:steps], rest[steps:2 * steps], rest[2 * steps:3 * steps]
    load_sem, send_sem, recv_sem = rest[3 * steps:]
    size = diag.shape[1]
    slots = offsets.shape[1]
    rows = t_cur.shape[0] // CHUNKS
    tree = n_vec == 2

    g, z, x, c = [lax.axis_index(name) for name in AXES]
    chips = n_atoms * n_vec
    place = z * n_vec + x

    def chip(step):
        at = lax.rem(place + step + chips, chips)
        return (g, at // n_vec, lax.rem(at, n_vec), c)

    mate = (g, z, x, 1 - c)
    far_ahead, far_behind = chip(2), chip(-2)
    if tree:
        near_ahead = near_behind = (g, z, 1 - x, c)
        partners = (mate, near_ahead, far_ahead, far_behind)
    else:
        near_ahead, near_behind = chip(1), chip(-1)
        partners = (mate, near_ahead, near_behind, far_ahead, far_behind)

    sources = (t_cur_hbm, offsets_hbm, stored_hbm.at[pl.ds(0, slots)],
               stored_hbm.at[pl.ds(slots, slots)], diag_hbm, t_prev_hbm)
    targets = (t_cur, offsets, stored.at[pl.ds(0, slots)],
               stored.at[pl.ds(slots + 1, slots)], diag, t_prev)
    loads = [
        pltpu.make_async_copy(source, target, load_sem.at[i])
        for i, (source, target) in enumerate(zip(sources, targets))
    ]
    for load in loads:
        load.start()

    barrier = pltpu.get_barrier_semaphore()
    for partner in partners:
        pl.semaphore_signal(barrier, inc=1, device_id=partner, device_id_type=MESH)
    for r in range(2):
        stored[r * (slots + 1) + slots] = jnp.zeros((size, size), BF16)

    def copies(s):
        window, out, arrive = windows[s], outgoing[s], incoming[s]

        def copy(which, src, dst, device):
            return pltpu.make_async_remote_copy(
                src_ref=src, dst_ref=dst, send_sem=send_sem.at[s, which],
                recv_sem=recv_sem.at[s, which], device_id=device, device_id_type=MESH,
            )

        near_src = 4 * (1 - x) if tree else 0
        at = lambda first: window.at[pl.ds(first, 2)]
        return {
            FAR: copy(FAR, at(0), at(4), far_behind),
            NEAR: copy(NEAR, at(near_src), at(2), near_behind),
            MATE_NEAR: copy(MATE_NEAR, at(2), at(6), mate),
            MATE_FAR: copy(MATE_FAR, at(4 * (1 - c)), at(8), mate),
            PART_NEAR: copy(PART_NEAR, out.at[0], arrive.at[0], mate),
            PART_FAR: copy(PART_FAR, out.at[1], arrive.at[1], mate),
            PART_X: copy(PART_X, out.at[2], arrive.at[2], near_ahead),
            PART_Z: copy(PART_Z, out.at[3], arrive.at[3], far_ahead),
        }

    every = [copies(s) for s in range(steps)]

    def only(condition, action):
        if tree:
            pl.when(condition)(action)
        else:
            action()

    def block(r, w):
        return table[r][w - r]

    def send_vectors(s, load):
        windows[s][0] = load(0).astype(BF16)
        windows[s][1] = load(1).astype(BF16)
        every[s][FAR].start()
        only(x == 1, every[s][NEAR].start)

    def part(s, first, second):
        total = None
        for r, at in ((0, first), (1, second)):
            if at is not None:
                term = jnp.dot(windows[s][r], stored[at], preferred_element_type=F32)
                total = term if total is None else total + term
        return total

    def mate_parts(s):
        out = outgoing[s]
        for i in range(2):
            out[0, i] = part(s, *[pick(block(r, 6 + i), block(r, 2 + i)) for r in range(2)]).astype(BF16)
        every[s][PART_NEAR].start()
        for i in range(2):
            out[1, i] = part(s, *[pick(block(r, 2 + i), block(r, 6 + i)) for r in range(2)]).astype(BF16)
        every[s][PART_FAR].start()

    def pick(even, odd):
        return jnp.where(c == 0, even, odd)

    def own_parts(s):
        for i in range(2):
            sums[s, i] = part(s, block(0, 4 + i), block(1, 4 + i))
        sums[s, 2] = part(s, block(0, 8), block(1, 8))
        sums[s, 3] = part(s, None, block(1, 9))

    def own_terms(s):
        own[s, 1] = part(s, block(0, 1), None) + jnp.dot(
            windows[s][1], diag[1], preferred_element_type=F32
        )
        own[s, 0] = jnp.dot(windows[s][0], diag[0], preferred_element_type=F32) + forward(
            s, 1, block(0, 1)
        )

    def forward(s, slot, at):
        return lax.dot_general(
            windows[s][slot], stored[at], (((1,), (1,)), ((), ())), preferred_element_type=F32
        )

    def join_parts(s):
        out, arrive = outgoing[s], incoming[s]
        every[s][PART_NEAR].wait_recv()
        for i in range(2):
            out[2, i] = (sums[s, i] + arrive[0, i].astype(F32)).astype(BF16)
        every[s][PART_X].start()
        every[s][PART_FAR].wait_recv()
        for i in range(2):
            extra = arrive[1, i].astype(F32)
            sums[s, 2 + i] = sums[s, 2 + i] + jnp.where(c == 0, extra, 0.0)
        only(x == 1, lambda: send_far_part(s, False))

    def send_far_part(s, add):
        out, arrive = outgoing[s], incoming[s]
        for i in range(2):
            total = sums[s, 2 + i]
            if add:
                total = total + arrive[2, i].astype(F32)
            out[3, i] = total.astype(BF16)
        every[s][PART_Z].start()

    def relay_vectors(s):
        every[s][FAR].wait_recv()
        if tree:
            pl.when(x == 0)(every[s][NEAR].start)
        every[s][MATE_FAR].start()

    def relay_parts(s, condition):
        if tree:
            @pl.when(jnp.logical_and(x == 0, condition))
            def _():
                every[s][PART_X].wait_recv()
                send_far_part(s, True)

    def add_pair(s, slot, at):
        for r in range(2):
            own[s, r] = own[s, r] + forward(s, slot, at[r][0]) + forward(s, slot + 1, at[r][1])

    def far_terms(s):
        own[s, 0] = own[s, 0] + forward(s, 4, block(0, 8))
        own[s, 1] = own[s, 1] + forward(s, 4, block(1, 8)) + forward(s, 5, block(1, 9))

    def spread_vectors(s):
        every[s][NEAR].wait_recv()
        every[s][MATE_NEAR].start()

    def near_terms(s):
        add_pair(s, 2, [[block(r, 4), block(r, 5)] for r in range(2)])

    def mate_far_terms(s):
        every[s][MATE_FAR].wait_recv()
        add_pair(s, 8, [[pick(block(r, 2 + i), block(r, 6 + i)) for i in range(2)] for r in range(2)])

    def mate_near_terms(s):
        every[s][MATE_NEAR].wait_recv()
        add_pair(s, 6, [[pick(block(r, 6 + i), block(r, 2 + i)) for i in range(2)] for r in range(2)])

    def finish(s, before, result, part_rows):
        arrive = incoming[s]
        only(x == 1, every[s][PART_X].wait_recv)
        every[s][PART_Z].wait_recv()
        for r in range(2):
            total = own[s, r] + arrive[3, r].astype(F32)
            total = total + jnp.where(c == 1, arrive[1, r].astype(F32), 0.0)
            near = arrive[2, r].astype(F32)
            total = total + (jnp.where(x == 1, near, 0.0) if tree else near)
            cols = pl.ds(r * size, size)
            result[part_rows, cols] = 2.0 * total - before[part_rows, cols]

    chunk_rows = [pl.ds(h * rows, rows) for h in range(CHUNKS)]
    first = list(range(CHUNKS))
    second = [CHUNKS + h for h in first]
    last = z == n_atoms - 1

    def columns(ref, h):
        return lambda r: ref[chunk_rows[h], pl.ds(r * size, size)]

    def middle(group):
        for s in group:
            relay_parts(s, last)
        for s in group:
            relay_vectors(s)
            relay_parts(s, jnp.logical_not(last))

    def gather(s):
        far_terms(s)
        spread_vectors(s)
        near_terms(s)
        mate_far_terms(s)
        mate_near_terms(s)

    loads[0].wait()
    pl.semaphore_wait(barrier, len(partners))
    for h in first:
        send_vectors(h, columns(t_cur, h))
    loads[1].wait()
    table = []
    for r in range(2):
        of_row = {}
        for offset in range(1, 2 * HOPS + 1):
            at = jnp.int32(slots)
            for k in range(slots):
                at = jnp.where(offsets[r, k] == offset, jnp.int32(k), at)
            of_row[offset] = at + r * (slots + 1)
        table.append(of_row)
    loads[2].wait()
    loads[3].wait()
    for h in first:
        mate_parts(h)
        own_parts(h)
        join_parts(h)
    loads[4].wait()
    for h in first:
        own_terms(h)
    loads[5].wait()
    middle(first)
    for h in first:
        gather(h)
        finish(h, t_prev, t_one, chunk_rows[h])
        s = second[h]
        send_vectors(s, columns(t_one, h))
        mate_parts(s)
        own_parts(s)
        join_parts(s)
        own_terms(s)
    middle(second)
    for h in first:
        gather(second[h])
        finish(second[h], t_cur, t_two, chunk_rows[h])
    for s in range(steps):
        for copy in every[s].values():
            copy.wait_send()


def deliver(one, two, one_out, two_out, held, sems):
    rows = one.shape[0] // PIECES
    stages = []
    for i, (source, target) in enumerate(((one, one_out), (two, two_out))):
        for p in range(PIECES):
            part = pl.ds(p * rows, rows)
            stages.append((
                pltpu.make_async_copy(source.at[part], held.at[i, part], sems.at[0, i, p]),
                pltpu.make_async_copy(held.at[i, part], target.at[part], sems.at[1, i, p]),
            ))
    for load, _ in stages:
        load.start()
    for load, store in stages:
        load.wait()
        store.start()
    for _, store in stages:
        store.wait()


def solution(mesh):
    n_atoms, n_vec = mesh.shape["atoms"], mesh.shape["vec"]

    def local(t_prev, t_cur, diag_blocks, upper_half_blocks, offsets):
        rows = t_cur.shape[0] // CHUNKS
        size = diag_blocks.shape[1]
        slots = offsets.shape[1]
        steps = 2 * CHUNKS
        vmem = pl.BlockSpec(memory_space=pltpu.VMEM)
        hbm = pl.BlockSpec(memory_space=pltpu.HBM)
        results = pl.pallas_call(
            functools.partial(kernel, n_atoms, n_vec),
            out_shape=(
                jax.ShapeDtypeStruct(t_cur.shape, F32), jax.ShapeDtypeStruct(t_cur.shape, F32)
            ),
            in_specs=[hbm] * 5,
            out_specs=(vmem, vmem),
            scratch_shapes=[
                pltpu.SMEM(offsets.shape, jnp.int32),
                pltpu.VMEM(t_cur.shape, F32),
                pltpu.VMEM(t_prev.shape, F32),
                pltpu.VMEM(diag_blocks.shape, BF16),
                pltpu.VMEM((2 * (slots + 1), size, size), BF16),
                pltpu.VMEM((steps, 4, rows, size), F32),
                pltpu.VMEM((steps, 2, rows, size), F32),
                *[pltpu.VMEM((2 * HOPS + 2, rows, size), BF16) for _ in range(steps)],
                *[pltpu.VMEM((4, 2, rows, size), BF16) for _ in range(2 * steps)],
                pltpu.SemaphoreType.DMA((6,)),
                pltpu.SemaphoreType.DMA((steps, 8)),
                pltpu.SemaphoreType.DMA((steps, 8)),
            ],
            compiler_params=pltpu.CompilerParams(
                collective_id=0, has_side_effects=True, vmem_limit_bytes=62 << 20
            ),
        )(offsets, t_cur, t_prev, diag_blocks, upper_half_blocks)
        return pl.pallas_call(
            deliver,
            out_shape=tuple(jax.ShapeDtypeStruct(a.shape, a.dtype) for a in results),
            in_specs=[pl.BlockSpec(memory_space=pl.ANY)] * 2,
            out_specs=(hbm, hbm),
            scratch_shapes=[pltpu.VMEM((2, *t_cur.shape), F32), pltpu.SemaphoreType.DMA((2, 2, PIECES))],
        )(*results)

    in_specs = (
        P("grp", ("atoms", "vec", "sub")),
        P("grp", ("atoms", "vec", "sub")),
        P(AXES, None, None),
        P(AXES, None, None),
        P(AXES, None),
    )
    out_specs = (P("grp", ("atoms", "vec", "sub")), P("grp", ("atoms", "vec", "sub")))
    return jax.shard_map(local, mesh=mesh, in_specs=in_specs, out_specs=out_specs, check_vma=False)
```

time: 43.1 us -> 40.6 us (0.942)
  local copies, waits for them, and re-layouts: 7.05 us -> 0 us
  Pallas kernels: 35.1 us -> 39.7 us
    unnamed x12 -> x0, local copies, waits for them, and re-layouts: 7.05 us -> none
    pallas_call x1, Pallas kernels: 35.1 us -> 37.7 us  [local(): pl.pallas_call(functools.partial(kernel, n_atoms, n_vec), out_shape=(jax....]
    pallas_call x0 -> x1, Pallas kernels: none -> 1.97 us  [local(): pl.pallas_call(deliver, out_shape=tuple((jax.ShapeDtypeStruct(a.shape, a....]
where the time goes in v2:
time: 40.6 us; the launch traced here: 40.3 us
  Pallas kernels  39.7 us (98%)
  between operations  0.64 us (2%)
    pallas_call x1, Pallas kernels, local(): pl.pallas_call(functools.partial(kernel, n_atoms, n_vec), out_shape=(jax....  37.7 us
    pallas_call x1, Pallas kernels, local(): pl.pallas_call(deliver, out_shape=tuple((jax.ShapeDtypeStruct(a.shape, a....  1.97 us

profile of v2, /device:TPU:0, one launch (start us, length us, event | category | flops | bytes accessed | tf_op | source)
XLA Modules:
  0.0 40.3 jit_solution(4169554385604303219)
XLA Ops:
  0.6 37.7 %shard_map.68 = (f32[128,768]{1,0:T(8,128)}, f32[128,768]{1,0:T(8,128)}) custom-call(s32[2,5]{1,0:T(2,128)} %offsets_hbm.1, f32[128,768]{1,0:T(8,128)} %t_cur_hbm.1, f32[128,768]{1,0:T(8,128)} %t_prev_hbm.1, bf16[2,384,384]{2,1,0:T(8,128)(2,1)} %diag_hbm.1, bf16[10,384,384]{2,1,0:T(8,128)(2,1)} %stored_hbm.1), custom_call_target="tpu_custom_call" | custom-call | tf_op jit(solution)/shard_map/pallas_call | solution.py:308
  38.4 2.0 %shard_map.69 = (f32[128,768]{1,0:T(8,128)}, f32[128,768]{1,0:T(8,128)}) custom-call(f32[128,768]{1,0:T(8,128)} %get-tuple-element.4.one, f32[128,768]{1,0:T(8,128)} %get-tuple-element.5.two), custom_call_target="tpu_custom_call" | custom-call | tf_op jit(solution)/shard_map/pallas_call | solution.py:333

commit v3 on v2

--- a/solution.py
+++ b/solution.py
@@ -9,7 +9,6 @@
 
 HOPS = 4
 CHUNKS = 2
-PIECES = 2
 AXES = ("grp", "atoms", "vec", "sub")
 MESH = pl.DeviceIdType.MESH
 F32 = jnp.float32
@@ -276,23 +275,15 @@
             copy.wait_send()
 
 
-def deliver(one, two, one_out, two_out, held, sems):
-    rows = one.shape[0] // PIECES
-    stages = []
-    for i, (source, target) in enumerate(((one, one_out), (two, two_out))):
-        for p in range(PIECES):
-            part = pl.ds(p * rows, rows)
-            stages.append((
-                pltpu.make_async_copy(source.at[part], held.at[i, part], sems.at[0, i, p]),
-                pltpu.make_async_copy(held.at[i, part], target.at[part], sems.at[1, i, p]),
-            ))
-    for load, _ in stages:
-        load.start()
-    for load, store in stages:
-        load.wait()
-        store.start()
-    for _, store in stages:
-        store.wait()
+def deliver(one, two, one_out, two_out, sems):
+    copies = [
+        pltpu.make_async_copy(one, one_out, sems.at[0]),
+        pltpu.make_async_copy(two, two_out, sems.at[1]),
+    ]
+    for copy in copies:
+        copy.start()
+    for copy in copies:
+        copy.wait()
 
 
 def solution(mesh):
@@ -327,15 +318,15 @@
                 pltpu.SemaphoreType.DMA((steps, 8)),
             ],
             compiler_params=pltpu.CompilerParams(
-                collective_id=0, has_side_effects=True, vmem_limit_bytes=62 << 20
+                collective_id=0, has_side_effects=True, vmem_limit_bytes=58 << 20
             ),
         )(offsets, t_cur, t_prev, diag_blocks, upper_half_blocks)
         return pl.pallas_call(
             deliver,
             out_shape=tuple(jax.ShapeDtypeStruct(a.shape, a.dtype) for a in results),
-            in_specs=[pl.BlockSpec(memory_space=pl.ANY)] * 2,
+            in_specs=[vmem] * 2,
             out_specs=(hbm, hbm),
-            scratch_shapes=[pltpu.VMEM((2, *t_cur.shape), F32), pltpu.SemaphoreType.DMA((2, 2, PIECES))],
+            scratch_shapes=[pltpu.SemaphoreType.DMA((2,))],
         )(*results)
 
     in_specs = (

time: 40.6 us -> 40.7 us (level)
  no operation moved by 1% of the time
where the time goes in v3:
time: 40.7 us; the launch traced here: 40.4 us
  Pallas kernels  39.7 us (98%)
  between operations  0.64 us (2%)
    pallas_call x1, Pallas kernels, local(): pl.pallas_call(functools.partial(kernel, n_atoms, n_vec), out_shape=(jax....  37.7 us
    pallas_call x1, Pallas kernels, local(): pl.pallas_call(deliver, out_shape=tuple((jax.ShapeDtypeStruct(a.shape, a....  2.01 us

profile of v3, /device:TPU:0, one launch (start us, length us, event | category | flops | bytes accessed | tf_op | source)
XLA Modules:
  0.0 40.4 jit_solution(17492848264754202632)
XLA Ops:
  0.6 37.7 %shard_map.68 = (f32[128,768]{1,0:T(8,128)}, f32[128,768]{1,0:T(8,128)}) custom-call(s32[2,5]{1,0:T(2,128)} %offsets_hbm.1, f32[128,768]{1,0:T(8,128)} %t_cur_hbm.1, f32[128,768]{1,0:T(8,128)} %t_prev_hbm.1, bf16[2,384,384]{2,1,0:T(8,128)(2,1)} %diag_hbm.1, bf16[10,384,384]{2,1,0:T(8,128)(2,1)} %stored_hbm.1), custom_call_target="tpu_custom_call" | custom-call | tf_op jit(solution)/shard_map/pallas_call | solution.py:299
  38.4 2.0 %shard_map.69 = (f32[128,768]{1,0:T(8,128)}, f32[128,768]{1,0:T(8,128)}) custom-call(f32[128,768]{1,0:T(8,128)} %get-tuple-element.4.one, f32[128,768]{1,0:T(8,128)} %get-tuple-element.5.two), custom_call_target="tpu_custom_call" | custom-call | tf_op jit(solution)/shard_map/pallas_call | solution.py:324
